TPU v7x, 32 devices: a whole 2x2x4 slice. The times are simulated.
32 devices in a mesh: grp: 2 (over x), feed: 16 (over z, y, core).
Axes of the slice: x: 2, y: 2, z: 4, core: 2. Of those that a mesh axis runs over, the one named last changes fastest.
Arguments:
- samples: bfloat16 [32, 256, 65536], P(('grp', 'feed')), parts along dimension 0, may hold values from -6 to 6
- pfb_taps: float32 [4, 8192], replicated, may hold values from -0.03125 to 0.03125
Outputs:
- visibility: float32 [16384, 4096], P(('grp', 'feed')), parts along dimension 0
There are 2 independent parts, one for each index of `grp`. A program takes and returns all parts, laid end to end along the dimension named above; an argument that names none is the same for every part. Nothing has to cross between parts.
All inputs are finite; a program needn't handle non-finite values.
Results may differ from a plain program's by a relative error of at most 0.004.
Values may be sent and summed in bfloat16 or wider, within the bound.
No kernel may reach another device: no remote copies, remote signals or barrier semaphores. Data moves between devices by JAX's collectives and lax.ppermute only.
A program may use at most 192 MiB of HBM per device.

v0:
```python
import math

import jax
import jax.numpy as jnp
from jax import lax
from jax.sharding import PartitionSpec as P

FIRST_CH = 1536
TIME_BLOCKS = 2
ROWS_DEV = 512


def passed_along(value, axis, steps):
    count = lax.axis_size(axis)
    first, last = (max(0, -steps), min(count, count - steps))
    return lax.ppermute(value, axis, [(source, source + steps) for source in range(first, last)])


def dft_matrix(fft_len, first_channel, channel_count):
    sample_ids = jnp.arange(fft_len, dtype=jnp.int32)
    channel_ids = first_channel + jnp.arange(channel_count, dtype=jnp.int32)
    phase = sample_ids[:, None] * channel_ids[None, :] % fft_len
    angle = phase.astype(jnp.float32) * (2.0 * math.pi / fft_len)
    return jnp.concatenate([jnp.cos(angle), -jnp.sin(angle)], axis=1)


def filter_sum(extended, pfb_taps, count):
    tap_count = pfb_taps.shape[0]
    total = jnp.zeros((extended.shape[0], count, extended.shape[2]), jnp.float32)
    for tap_index in range(tap_count):
        total = (
            total
            + extended[:, tap_index : tap_index + count].astype(jnp.float32) * pfb_taps[tap_index]
        )
    return total


def apply_table(filtered, dft_table):
    feed_count, count, fft_len = filtered.shape
    product = jnp.dot(
        filtered.reshape(feed_count * count, fft_len),
        dft_table,
        precision=lax.Precision.HIGHEST,
        preferred_element_type=jnp.float32,
    )
    return product.reshape(feed_count, count, -1)


def body(samples, pfb_taps):
    feed_count = samples.shape[1]
    tap_count, fft_len = pfb_taps.shape
    frame_count = samples.shape[2] // fft_len
    devices = lax.axis_size("feed")
    my_index = lax.axis_index("feed")
    group_span = devices // TIME_BLOCKS
    total_feeds = feed_count * group_span
    channels = devices * ROWS_DEV // total_feeds
    owners = total_feeds // ROWS_DEV
    spectra_count = TIME_BLOCKS * frame_count
    later_block = my_index >= group_span
    frames = samples.reshape(feed_count, frame_count, fft_len)
    dft_table = dft_matrix(fft_len, FIRST_CH, channels)
    edge = tap_count - 1
    tail_frames = frames[:, frame_count - edge :]
    shifted = passed_along(tail_frames, "feed", group_span)
    before = jnp.where(later_block, shifted, jnp.zeros_like(shifted))
    extended = jnp.concatenate([before, frames], axis=1)
    spectra = apply_table(filter_sum(extended, pfb_taps, frame_count), dft_table)
    spectra = spectra.astype(jnp.bfloat16)
    per_channel = jnp.transpose(spectra.reshape(feed_count, frame_count, 2, channels), (3, 0, 2, 1))
    outgoing_all = jnp.repeat(
        per_channel.reshape(channels, feed_count, 2 * frame_count), owners, axis=0
    )
    gathered = lax.all_to_all(outgoing_all, "feed", split_axis=0, concat_axis=0, tiled=True)
    arranged = gathered.reshape(TIME_BLOCKS, group_span, feed_count, 2, frame_count)
    all_feeds = jnp.transpose(arranged, (1, 2, 3, 0, 4)).reshape(total_feeds, 2 * spectra_count)
    real_part = all_feeds[:, :spectra_count]
    imag_part = all_feeds[:, spectra_count:]
    right_matrix = jnp.concatenate(
        [all_feeds, jnp.concatenate([-imag_part, real_part], axis=1)], axis=0
    ).T
    row_start = my_index % owners * ROWS_DEV
    left_rows = lax.dynamic_slice_in_dim(all_feeds, row_start, ROWS_DEV, 0)
    visibility = jnp.dot(left_rows, right_matrix, preferred_element_type=jnp.float32) * (
        1.0 / spectra_count
    )
    return visibility


def solution(mesh):
    placed = (P(("grp", "feed"), None, None), P())
    return jax.shard_map(
        body, mesh=mesh, in_specs=placed, out_specs=P(("grp", "feed"), None), check_vma=False
    )
```

profile of v0, /device:TPU:0, one launch (start us, length us, event | category | flops | bytes accessed | tf_op | source)
XLA Modules:
  0.0 726.7 jit_solution(738564118373659306)
XLA Ops:
  0.0 29.2 %copy.11 = bf16[32,8,8,8192]{3,2,1,0:T(8,128)(2,1)} copy(bf16[32,8,8,8192]{3,1,2,0:T(8,128)(2,1)} %bitcast.30) | data formatting | bytes 67108864
  29.2 0.0 copy-start
  29.2 29.4 %copy.6 = bf16[256,8,8192]{2,0,1:T(8,128)(2,1)} copy(bf16[256,8,8192]{2,1,0:T(8,128)(2,1)} %bitcast.29) | data formatting | bytes 67108864 | tf_op jit(solution)/shard_map/reshape | solution.py:61
  58.6 10.5 %slice.40 = bf16[256,3,8192]{2,0,1:T(8,128)(2,1)} slice(bf16[256,8,8192]{2,0,1:T(8,128)(2,1)} %copy.6), slice={[0:256], [5:8], [0:8192]} | slice | bytes 25165824 | tf_op jit(solution)/shard_map/slice | solution.py:64
  69.1 10.4 %collective-permute-start = (bf16[256,3,8192]{2,0,1:T(8,128)(2,1)}, bf16[256,3,8192]{2,0,1:T(8,128)(2,1)}, u32[]{:S(2)}, u32[]{:S(2)}) collective-permute-start(bf16[256,3,8192]{2,0,1:T(8,128)(2,1)} %slice.40), channel_id=1, source_target_pairs={{0,8},{1,9},{2,10},{3,11},{4,12},{5,13},{6,14},{7,15},{16,24},{17,... | collective-permute-start | bytes 37748744 | tf_op jit(solution)/shard_map/ppermute | solution.py:16
  79.5 0.0 copy-done
  79.5 0.1 fusion.40
  79.6 1.2 fusion.34
  80.8 264.1 %collective-permute-done = bf16[256,3,8192]{2,0,1:T(8,128)(2,1)} collective-permute-done((bf16[256,3,8192]{2,0,1:T(8,128)(2,1)}, bf16[256,3,8192]{2,0,1:T(8,128)(2,1)}, u32[]{:S(2)}, u32[]{:S(2)}) %collective-permute-start) | collective-permute-done | bytes 12582944 | tf_op jit(solution)/shard_map/ppermute | solution.py:16
  345.0 1.0 broadcast_select_fusion
  345.9 86.0 %fusion.21 = bf16[256,8,8]{0,2,1:T(8,128)(2,1)S(1)} fusion(bf16[256,8,8192]{2,0,1:T(8,128)(2,1)} %copy.6, bf16[256,3,8192]{2,0,1:T(8,128)(2,1)S(1)} %broadcast_select_fusion, f32[8192]{0:T(1024)S(1)} %bitcast.38, f32[8192]{0:T(1024)S(1)} %bitcast.39, f32[8192]{0:T(1024)S(1)} %bitcast.37, f32[8192]{0:T(1024)S(1)} %bitcast.36, ...), kind=kOutput, calls=%fused_computation.26 | convolution fusion | flops 1845575680 | bytes 46563328 | tf_op jit(solution)/shard_map/dot_general | solution.py:40
  431.9 0.7 broadcast_in_dim.9
  432.6 281.4 %all-to-all-start = ((bf16[16,256,16]{1,2,0:T(8,128)(2,1)}), bf16[16,256,16]{1,2,0:T(8,128)(2,1)S(1)}, u32[]{:S(2)}, u32[]{:S(2)}) async-start(bf16[16,256,16]{1,2,0:T(8,128)(2,1)} %bitcast.7), calls=%async_computation | async-start | bytes 262144 | tf_op jit(solution)/shard_map/all_to_all | solution.py:74
  714.0 7.9 %all-to-all-done = bf16[16,256,16]{1,2,0:T(8,128)(2,1)S(1)} async-done(((bf16[16,256,16]{1,2,0:T(8,128)(2,1)}), bf16[16,256,16]{1,2,0:T(8,128)(2,1)S(1)}, u32[]{:S(2)}, u32[]{:S(2)}) %all-to-all-start) | async-done | bytes 131104 | tf_op jit(solution)/shard_map/all_to_all | solution.py:74
  722.0 4.7 convolution_multiply_fusion
  (6 shorter events, 0.1 us)
Async XLA Ops:
  29.2 50.3 %copy-start = (f32[4,8192]{1,0:T(4,128)S(1)}, f32[4,8192]{1,0:T(4,128)}, u32[]{:S(2)}) copy-start(f32[4,8192]{1,0:T(4,128)} %param.3) | copy-start | bytes 393220
  69.1 275.9 %collective-permute-start = (bf16[256,3,8192]{2,0,1:T(8,128)(2,1)}, bf16[256,3,8192]{2,0,1:T(8,128)(2,1)}, u32[]{:S(2)}, u32[]{:S(2)}) collective-permute-start(bf16[256,3,8192]{2,0,1:T(8,128)(2,1)} %slice.40), channel_id=1, source_target_pairs={{0,8},{1,9},{2,10},{3,11},{4,12},{5,13},{6,14},{7,15},{16,24},{17,... | collective-permute-start | bytes 37748744 | tf_op jit(solution)/shard_map/ppermute | solution.py:16
  432.6 289.3 %all-to-all-start = ((bf16[16,256,16]{1,2,0:T(8,128)(2,1)}), bf16[16,256,16]{1,2,0:T(8,128)(2,1)S(1)}, u32[]{:S(2)}, u32[]{:S(2)}) async-start(bf16[16,256,16]{1,2,0:T(8,128)(2,1)} %bitcast.7), calls=%async_computation | async-start | bytes 262144 | tf_op jit(solution)/shard_map/all_to_all | solution.py:74
where the time goes:
time: 727 us
  starting transfers between devices  292 us (40%)
  waiting for transfers between devices  272 us (37%)
  matrix products  90.6 us (12%)
  local copies, waits for them, and re-layouts  69.9 us (10%)
    all_to_all x1, starting transfers between devices, body(): lax.all_to_all(outgoing_all, 'feed', split_axis=0, concat_axis=0, tiled=T...  281 us
    ppermute x1, waiting for transfers between devices, passed_along(): lax.ppermute(value, axis, [(source, source + steps) for source in range(f...  264 us
    dot_general x1, matrix products, apply_table(): jnp.dot(filtered.reshape(feed_count * count, fft_len), dft_table, precisi...  86 us
    reshape x1, local copies, waits for them, and re-layouts, body(): frames = samples.reshape(feed_count, frame_count, fft_len)  29.4 us
    unnamed x4, local copies, waits for them, and re-layouts  29.2 us
  transfers between devices with their start and end apart: 2, of which 2 were waited for; matrix products, arithmetic and copies ran while one was open for 0% of the time, Pallas kernels for 0%

commit v1 on v0

v1 whole, which is shorter than its diff:
```python
import functools
import math

import jax
import jax.numpy as jnp
import numpy as np
from jax import lax
from jax.experimental import pallas as pl
from jax.experimental.pallas import tpu as pltpu
from jax.sharding import PartitionSpec as P

FIRST_CH = 1536
TIME_BLOCKS = 2
ROWS_DEV = 512
PIECES = 2


def dft_rows(fft_len, first_channel, channel_count):
    sample_ids = np.arange(fft_len, dtype=np.int64)
    channel_ids = first_channel + np.arange(channel_count, dtype=np.int64)
    phase = channel_ids[:, None] * sample_ids[None, :] % fft_len
    angle = phase.astype(np.float64) * (2.0 * math.pi / fft_len)
    return np.concatenate([np.cos(angle), -np.sin(angle)], axis=0).astype(np.float32)


def spectra_kernel(
    group_span, owners, x_hbm, taps_ref, dft_ref, out_ref, x_buf, table, parts, sems
):
    tap_count, fft_len = taps_ref.shape
    columns = dft_ref.shape[0]
    channels = columns // 2
    frame_count = x_hbm.shape[2] // fft_len
    piece = fft_len // PIECES
    edge = tap_count - 1
    width = tap_count * columns
    later_block = lax.axis_index("feed") >= group_span

    def fetch(index):
        span = pl.ds(index * piece, piece)
        return pltpu.make_async_copy(x_hbm.at[0, :, span], x_buf.at[:, span], sems.at[index])

    for index in range(frame_count * PIECES):
        fetch(index).start()

    step = 1024
    for start in range(0, fft_len, step):
        dft = dft_ref[:, start : start + step]
        scaled = jnp.concatenate(
            [taps_ref[m : m + 1, start : start + step] * dft for m in range(tap_count)], axis=0
        )
        high = scaled.astype(jnp.bfloat16).astype(jnp.float32)
        both = jnp.concatenate([high, scaled - high], axis=0)
        table[start : start + step, :] = both.T.astype(jnp.bfloat16)

    window = [None] * (frame_count + edge)
    for frame in range(frame_count):
        total = None
        for p in range(PIECES):
            fetch(frame * PIECES + p).wait()
            start = frame * fft_len + p * piece
            product = jnp.dot(
                x_buf[:, start : start + piece],
                table[p * piece : (p + 1) * piece, :],
                preferred_element_type=jnp.float32,
            )
            total = product if total is None else total + product
        turned = total.T
        summed = turned[:width] + turned[width:]
        for m in range(tap_count):
            term = summed[m * columns : (m + 1) * columns]
            spot = frame + edge - m
            window[spot] = term if window[spot] is None else window[spot] + term
    for spot in range(frame_count + edge):
        parts[:, spot, :] = window[spot]

    for c in range(channels):
        now = jnp.concatenate([parts[c, :frame_count], parts[channels + c, :frame_count]], axis=0)
        high = now.astype(jnp.bfloat16)
        low = now - high.astype(jnp.float32)
        low = jnp.concatenate([low[:4], low[frame_count : frame_count + 4]], axis=0)
        tail = jnp.concatenate(
            [parts[c, frame_count : frame_count + 4], parts[channels + c, frame_count : frame_count + 4]],
            axis=0,
        )
        sublane = lax.broadcasted_iota(jnp.int32, tail.shape, 0)
        tail = jnp.where(sublane % 4 < edge, tail, 0.0)
        tail_high = tail.astype(jnp.bfloat16).astype(jnp.float32)
        tail_low = tail - tail_high
        extra = jnp.concatenate(
            [jnp.where(later_block, low, tail_high), jnp.where(later_block, 0.0, tail_low)], axis=0
        ).astype(jnp.bfloat16)
        whole = jnp.concatenate([high, extra], axis=0)
        for o in range(owners):
            out_ref[c * owners + o] = whole


def correlate_kernel(scale, owners, got_ref, out_ref, right, left, turned):
    devices, rows, feed_count = got_ref.shape
    group_span = devices // TIME_BLOCKS
    frame_count = rows // 4
    depth = right.shape[0]
    block_rows = out_ref.shape[0]
    total_feeds = right.shape[1]

    @pl.when(pl.program_id(0) == 0)
    def _():
        for g in range(group_span):
            span = slice(g * feed_count, (g + 1) * feed_count)
            first = got_ref[g].astype(jnp.float32)
            second = got_ref[group_span + g].astype(jnp.float32)
            extra = (
                first[2 * frame_count : 3 * frame_count]
                + first[3 * frame_count :]
                + second[2 * frame_count : 3 * frame_count]
            )
            zero = jnp.zeros((frame_count - 4, feed_count), jnp.float32)
            extra = jnp.concatenate([extra[:4], zero, extra[4:8], zero], axis=0)
            fixed = second[: 2 * frame_count] + extra
            right[: 2 * frame_count, span] = got_ref[g, : 2 * frame_count]
            right[2 * frame_count :, span] = fixed.astype(jnp.bfloat16)
        row_start = lax.axis_index("feed") % owners * ROWS_DEV
        mine = right[:, pl.ds(pl.multiple_of(row_start, ROWS_DEV), ROWS_DEV)].astype(jnp.float32)
        halves = [mine[k * frame_count : (k + 1) * frame_count] for k in range(4)]
        swapped = jnp.concatenate([halves[1], -halves[0], halves[3], -halves[2]], axis=0)
        left[...] = mine.T.astype(jnp.bfloat16)
        turned[...] = swapped.T.astype(jnp.bfloat16)

    span = pl.ds(pl.multiple_of(pl.program_id(0) * block_rows, block_rows), block_rows)
    out_ref[:, :total_feeds] = (
        jnp.dot(left[span, :], right[...], preferred_element_type=jnp.float32) * scale
    )
    out_ref[:, total_feeds:] = (
        jnp.dot(turned[span, :], right[...], preferred_element_type=jnp.float32) * scale
    )


def body(samples, pfb_taps):
    feed_count = samples.shape[1]
    tap_count, fft_len = pfb_taps.shape
    frame_count = samples.shape[2] // fft_len
    devices = lax.axis_size("feed")
    group_span = devices // TIME_BLOCKS
    total_feeds = feed_count * group_span
    channels = devices * ROWS_DEV // total_feeds
    owners = total_feeds // ROWS_DEV
    spectra_count = TIME_BLOCKS * frame_count
    columns = 2 * channels
    rows = 4 * frame_count
    dft = jnp.asarray(dft_rows(fft_len, FIRST_CH, channels))
    in_vmem = pl.BlockSpec(memory_space=pltpu.VMEM)
    outgoing = pl.pallas_call(
        functools.partial(spectra_kernel, group_span, owners),
        out_shape=jax.ShapeDtypeStruct((devices, rows, feed_count), jnp.bfloat16),
        in_specs=[pl.BlockSpec(memory_space=pl.ANY), in_vmem, in_vmem],
        out_specs=in_vmem,
        scratch_shapes=[
            pltpu.VMEM((feed_count, samples.shape[2]), jnp.bfloat16),
            pltpu.VMEM((fft_len, 2 * tap_count * columns), jnp.bfloat16),
            pltpu.VMEM((columns, 2 * frame_count, feed_count), jnp.float32),
            pltpu.SemaphoreType.DMA((frame_count * PIECES,)),
        ],
        compiler_params=pltpu.CompilerParams(vmem_limit_bytes=56 * 2**20),
        name="spectra",
    )(samples, pfb_taps, dft)
    gathered = lax.all_to_all(outgoing, "feed", split_axis=0, concat_axis=0, tiled=True)
    block_rows = 64
    return pl.pallas_call(
        functools.partial(correlate_kernel, 1.0 / spectra_count, owners),
        out_shape=jax.ShapeDtypeStruct((ROWS_DEV, 2 * total_feeds), jnp.float32),
        grid=(ROWS_DEV // block_rows,),
        in_specs=[pl.BlockSpec((devices, rows, feed_count), lambda i: (0, 0, 0))],
        out_specs=pl.BlockSpec((block_rows, 2 * total_feeds), lambda i: (i, 0)),
        scratch_shapes=[
            pltpu.VMEM((rows, total_feeds), jnp.bfloat16),
            pltpu.VMEM((ROWS_DEV, rows), jnp.bfloat16),
            pltpu.VMEM((ROWS_DEV, rows), jnp.bfloat16),
        ],
        compiler_params=pltpu.CompilerParams(vmem_limit_bytes=32 * 2**20),
        name="correlate",
    )(gathered)


def solution(mesh):
    placed = (P(("grp", "feed"), None, None), P())
    return jax.shard_map(
        body, mesh=mesh, in_specs=placed, out_specs=P(("grp", "feed"), None), check_vma=False
    )
```

time: 727 us -> 39.7 us (0.05)
  starting transfers between devices: 292 us -> 0 us
  waiting for transfers between devices: 272 us -> 0 us
  matrix products: 90.6 us -> 0 us
  local copies, waits for them, and re-layouts: 69.9 us -> 0 us
  Pallas kernels: 0 us -> 22 us
  blocking collectives: 0 us -> 17.4 us
    all_to_all x1 -> x0, starting transfers between devices: 281 us -> none  [body(): lax.all_to_all(outgoing_all, 'feed', split_axis=0, concat_axis=0, tiled=T...]
    ppermute x1 -> x0, waiting for transfers between devices: 264 us -> none  [passed_along(): lax.ppermute(value, axis, [(source, source + steps) for source in range(f...]
    dot_general x2 -> x0, matrix products: 90.6 us -> none  [the longest x1 86 us: apply_table(): jnp.dot(filtered.reshape(feed_count * count, fft_len), dft_table, precisi...]
    reshape x3 -> x0, local copies, waits for them, and re-layouts: 29.4 us -> none  [the longest x1 29.4 us: body(): frames = samples.reshape(feed_count, frame_count, fft_len)]
    unnamed x4 -> x0, local copies, waits for them, and re-layouts: 29.2 us -> none
    pallas_call x0 -> x2, Pallas kernels: none -> 22 us  [the longest x1 16.5 us: body(): pl.pallas_call(functools.partial(spectra_kernel, group_span, owners), out...]
    all_to_all x0 -> x1, blocking collectives: none -> 17.4 us  [body(): lax.all_to_all(outgoing, 'feed', split_axis=0, concat_axis=0, tiled=True)]
    slice x2 -> x0, local copies, waits for them, and re-layouts: 10.6 us -> none  [the longest x1 10.5 us: body(): tail_frames = frames[:, frame_count - edge:]]
  transfers between devices with their start and end apart: 2 -> 0, of which waited for: 2 -> 0; matrix products, arithmetic and copies ran while one was open for 0% -> 0% of each run, Pallas kernels for 0% -> 0%
where the time goes in v1:
time: 39.7 us; the launch traced here: 39.4 us
  Pallas kernels  22 us (55%)
  blocking collectives  17.4 us (44%)
    all_to_all x1, blocking collectives, body(): lax.all_to_all(outgoing, 'feed', split_axis=0, concat_axis=0, tiled=True)  17.4 us
    pallas_call x1, Pallas kernels, body(): pl.pallas_call(functools.partial(spectra_kernel, group_span, owners), out...  16.5 us
    pallas_call x1, Pallas kernels, body(): pl.pallas_call(functools.partial(correlate_kernel, 1.0 / spectra_count, o...  5.49 us

profile of v1, /device:TPU:0, one launch (start us, length us, event | category | flops | bytes accessed | tf_op | source)
XLA Modules:
  0.0 39.4 jit_solution(17198658152910279320)
XLA Ops:
  0.0 16.5 %spectra.1 = bf16[16,32,256]{2,1,0:T(8,128)(2,1)} custom-call(bf16[1,256,65536]{2,1,0:T(8,128)(2,1)} %x_hbm.1, f32[4,8192]{1,0:T(4,128)} %taps_ref.1, f32[8,8192]{1,0:T(8,128)} %constant.2.clone.dft_ref), custom_call_target="tpu_custom_call" | custom-call | tf_op jit(solution)/shard_map/spectra/pallas_call | solution.py:151
  16.5 17.4 %all_to_all.5.got_ref = bf16[16,32,256]{2,1,0:T(8,128)(2,1)S(1)} all-to-all(bf16[16,32,256]{2,1,0:T(8,128)(2,1)} %spectra.1), channel_id=1, replica_groups=mesh['grp'=2,'feed'=16] {'feed'}, dimensions={0} | all-to-all | bytes 524288 | tf_op jit(solution)/shard_map/all_to_all | solution.py:165
  33.9 5.5 %correlate.1 = f32[512,4096]{1,0:T(8,128)} custom-call(bf16[16,32,256]{2,1,0:T(8,128)(2,1)S(1)} %all_to_all.5.got_ref), custom_call_target="tpu_custom_call" | custom-call | tf_op jit(solution)/shard_map/correlate/pallas_call | solution.py:167
